TPU v7x, 512 devices: a whole 4x4x16 slice. The times are simulated.
512 devices in a mesh: dp: 64 (over y, z), segment: 2 (over core), mp: 4 (over x).
Axes of the slice: x: 4, y: 4, z: 16, core: 2. Of those that a mesh axis runs over, the one named last changes fastest.
Arguments:
- hidden: bfloat16 [2, 512, 4096], P('segment', ('dp', 'mp')), may hold values from -6 to 6
- gain: float32 [4096], replicated, may hold values from 0.5 to 1.5
- head: bfloat16 [4096, 131072], P('segment', ('dp', 'mp')), may hold values from -0.09375 to 0.09375
- queries: bfloat16 [8, 131072], P(None, ('dp', 'mp')), may hold values from -48 to 48
- doc_spans: int32 [8], replicated, may hold values from 1 to 4, as said below
- labels: int32 [8], replicated, may hold values from 0 to 7
Outputs:
- grad_head: bfloat16 [4096, 131072], P('segment', ('dp', 'mp'))
- loss: float32 [], replicated
Inputs may be any that keep to these rules, and one draw needn't show every extreme that they name: `doc_spans`: the counts sum to 16; documents own consecutive spans in order; at least two documents have 4 spans.
All inputs are finite; a program needn't handle non-finite values.
Results may differ from a plain program's by a relative error of at most 0.008.
Values may be sent and summed in bfloat16 or wider, within the bound.
A program may use at most 64 MiB of HBM per device.

v0:
```python
import math
import jax
import jax.numpy as jnp
from jax import lax
from jax.sharding import PartitionSpec as P

V_DEV = 512
CH_MB = 8
NDOC = 8


def saturate(logits):
    return jnp.log1p(jax.nn.softplus(logits))


def slope(logits):
    return jax.nn.sigmoid(logits) / (1.0 + jax.nn.softplus(logits))


def row_norm(hidden, gain):
    values = hidden.astype(jnp.float32)
    mean_sq = jnp.mean(values * values, axis=-1, keepdims=True)
    return (values * lax.rsqrt(mean_sq + 1e-05) * gain).astype(jnp.bfloat16)


def owned_by(span_ids, bounds):
    inside = (span_ids[:, None] >= bounds[None, :-1]) & (span_ids[:, None] < bounds[None, 1:])
    return inside.astype(jnp.float32)


def shards(hidden, gain, head, queries, doc_spans, labels):
    width_dp = lax.axis_size("dp")
    width_mp = lax.axis_size("mp")
    segments = lax.axis_size("segment")
    vocab = V_DEV * width_dp * width_mp
    rows_here = hidden.shape[1]
    tok_mb = rows_here * width_dp * width_mp
    span = tok_mb // CH_MB
    micro_index = lax.axis_index("segment")
    normed = row_norm(hidden, gain)
    head_full = lax.all_gather(head, "segment", axis=0, tiled=True)
    bounds = jnp.concatenate([jnp.zeros((1,), jnp.int32), jnp.cumsum(doc_spans)])
    query_values = queries.astype(jnp.float32)
    scale = 1.0 / (math.sqrt(vocab) * span)

    def doc_table(count):
        span_ids = (micro_index * tok_mb + jnp.arange(count, dtype=jnp.int32)) // span
        return owned_by(span_ids, bounds)

    table = doc_table(tok_mb)
    rows = lax.all_gather(normed, ("dp", "mp"), axis=1, tiled=True)[0]
    block = jnp.dot(rows, head_full, preferred_element_type=jnp.float32)
    local_table = doc_table(rows.shape[0])
    pooled_now = jnp.dot(local_table.T, saturate(block), precision=lax.Precision.HIGHEST)
    pooled = pooled_now
    pooled = lax.psum(pooled, "segment")
    terms = jnp.dot(query_values, pooled.T, precision=lax.Precision.HIGHEST)
    scores = lax.psum(terms, ("dp", "mp")) * scale
    row_top = jnp.max(scores, axis=1, keepdims=True)
    log_total = row_top + jnp.log(jnp.sum(jnp.exp(scores - row_top), axis=1, keepdims=True))
    picks = (labels[:, None] == jnp.arange(NDOC, dtype=jnp.int32)[None, :]).astype(jnp.float32)
    loss = jnp.sum(log_total[:, 0] - jnp.sum(scores * picks, axis=1))
    score_grad = jnp.exp(scores - log_total) - picks
    pooled_grad = scale * jnp.dot(score_grad.T, query_values, precision=lax.Precision.HIGHEST)
    token_grad = jnp.dot(table, pooled_grad, precision=lax.Precision.HIGHEST)
    grad_scale = math.sqrt(vocab) * span / math.sqrt(segments * tok_mb)
    logit_grad = (token_grad * slope(block) * grad_scale).astype(jnp.bfloat16)
    rows = lax.all_gather(normed, ("dp", "mp"), axis=1, tiled=True)[0]
    summed = lax.dot_general(
        rows, logit_grad, (((0,), (0,)), ((), ())), preferred_element_type=jnp.float32
    )
    grad_head = lax.psum_scatter(
        summed.astype(jnp.bfloat16), "segment", scatter_dimension=0, tiled=True
    )
    return (grad_head, loss)


def solution(mesh):
    return jax.shard_map(
        shards,
        mesh=mesh,
        in_specs=(
            P("segment", ("dp", "mp"), None),
            P(),
            P("segment", ("dp", "mp")),
            P(None, ("dp", "mp")),
            P(),
            P(),
        ),
        out_specs=(P("segment", ("dp", "mp")), P()),
        check_vma=False,
    )
```

profile of v0, /device:TPU:1, one launch (start us, length us, event | category | flops | bytes accessed | tf_op | source)
XLA Modules:
  0.0 1000.5 jit_solution(7330918718881482748)
XLA Ops:
  7.2 0.0 copy-start
  7.2 0.0 all-gather.5.cloned.1.call-start
  7.2 0.7 all-gather.5.cloned.1.call-update
  7.9 0.0 all-gather.3.cloned.1.call-start
  8.0 0.9 fusion.16
  8.8 0.8 fusion.18
  9.7 0.6 copy.10
  10.3 0.0 all-gather.3.cloned.1.call-update
  10.3 0.0 reduce-scatter.2.cloned.1.call-start
  10.4 0.8 reduce-window.8
  11.2 0.1 pad_add_fusion
  11.3 29.7 %all-gather.5.cloned.1.call-done = bf16[4096,512]{1,0:T(8,128)(2,1)} async-done(((bf16[2048,512]{1,0:T(8,128)(2,1)}), bf16[4096,512]{1,0:T(8,128)(2,1)}) %all-gather.5.cloned.1.call-update) | async-done | bytes 4194320 | tf_op jit(solution)/shard_map/all_gather | solution.py:41
  41.0 216.8 %all-gather.3.cloned.1.call-done = bf16[1,512,4096]{2,0,1:T(2,128)(2,1)} async-done(((bf16[1,2,4096]{2,0,1:T(2,128)(2,1)}), bf16[1,512,4096]{2,0,1:T(2,128)(2,1)}) %all-gather.3.cloned.1.call-update) | async-done | bytes 4194320 | tf_op jit(solution)/shard_map/all_gather | solution.py:68
  257.8 9.3 fusion.1
  267.1 1.4 fusion.7
  268.5 11.3 %psum.14 = f32[8,512]{1,0:T(8,128)S(1)} all-reduce(f32[8,512]{1,0:T(8,128)S(1)} %fusion.7), channel_id=1, replica_groups=mesh['dp'=64,'segment'=2,'mp'=4] {'segment'}, use_global_device_ids=true, to_apply=%region_2.3 | all-reduce | flops 4096 | bytes 32768 | tf_op jit(solution)/shard_map/psum | solution.py:56
  279.7 0.1 convolution_bitcast_fusion
  279.9 577.1 %psum.15 = f32[8,8]{0,1:T(8,128)S(1)} all-reduce(f32[8,8]{0,1:T(8,128)S(1)} %convolution_bitcast_fusion), channel_id=1, replica_groups=mesh['dp'=64,'segment'=2,'mp'=4] {'dp','mp'}, use_global_device_ids=true, to_apply=%region_3.4 | all-reduce | flops 64 | bytes 512 | tf_op jit(solution)/shard_map/psum | solution.py:58
  857.0 0.6 subtract_reduce_fusion
  857.6 0.1 convolution_multiply_fusion.1
  857.7 1.4 fusion.6
  859.1 14.9 %convolution_convert_fusion = bf16[4096,512]{1,0:T(8,128)(2,1)} fusion(bf16[512,512]{1,0:T(8,128)(2,1)S(1)} %fusion.6, bf16[1,512,4096]{2,0,1:T(2,128)(2,1)} %all-gather.3.cloned.1.call-done), kind=kOutput, calls=%fused_computation | convolution fusion | flops 2149580800 | bytes 8912896 | tf_op jit(solution)/shard_map/dot_general | solution.py:69
  874.0 0.0 reduce-scatter.2.cloned.1.call-update
  874.0 119.9 %reduce-scatter.2.cloned.1.call-done = bf16[2048,512]{1,0:T(8,128)(2,1)} async-done(((bf16[4096,512]{1,0:T(8,128)(2,1)}), bf16[2048,512]{1,0:T(8,128)(2,1)}) %reduce-scatter.2.cloned.1.call-update) | async-done | bytes 2097168 | tf_op jit(solution)/shard_map/reduce_scatter | solution.py:72
  (7 shorter events, 0.1 us)
Async XLA Ops:
  7.2 272.6 %copy-start = (bf16[8,512]{1,0:T(8,128)(2,1)S(1)}, bf16[8,512]{1,0:T(8,128)(2,1)}, u32[]{:S(2)}) copy-start(bf16[8,512]{1,0:T(8,128)(2,1)} %param.9) | copy-start | bytes 24580
  7.2 33.8 %all-gather.5.cloned.1.call-start = ((), (), s32[]{:S(2)}) async-start(), calls=%async_computation.2 | async-start | bytes 6291456 | tf_op jit(solution)/shard_map/all_gather | solution.py:41
  7.9 249.9 %all-gather.3.cloned.1.call-start = ((), (), s32[]{:S(2)}) async-start(), calls=%async_computation.1 | async-start | bytes 8421376 | tf_op jit(solution)/shard_map/all_gather | solution.py:68
  10.3 983.7 %reduce-scatter.2.cloned.1.call-start = ((), (), s32[]{:S(2)}) async-start(), calls=%async_computation.3 | async-start | bytes 6291456 | tf_op jit(solution)/shard_map/reduce_scatter | solution.py:72
  11.3 845.7 %copy-start.1 = (s32[8]{0:T(128)S(1)}, s32[8]{0:T(128)}, u32[]{:S(2)}) copy-start(s32[8]{0:T(128)} %param.11) | copy-start | bytes 100
Sparse Core Ops, SparseCore 0:
  10.1 30.8 all-gather.4
  46.2 211.6 all-gather.2
  874.2 119.7 reduce-scatter.1
where the time goes:
time: 1000 us
  blocking collectives  588 us (59%)
  waiting for transfers between devices  367 us (37%)
  matrix products  27.1 us (3%)
  between operations  13.8 us (1%)
    psum x1, blocking collectives, shards(): scores = lax.psum(terms, ('dp', 'mp')) * scale  577 us
    all_gather x1, waiting for transfers between devices, shards(): rows = lax.all_gather(normed, ('dp', 'mp'), axis=1, tiled=True)[0]  217 us
    reduce_scatter x1, waiting for transfers between devices, shards(): lax.psum_scatter(summed.astype(jnp.bfloat16), 'segment', scatter_dimensio...  120 us
    all_gather x1, waiting for transfers between devices, shards(): head_full = lax.all_gather(head, 'segment', axis=0, tiled=True)  29.7 us
  transfers between devices with their start and end apart: 3, of which 3 were waited for; matrix products, arithmetic and copies ran while one was open for 0% of the time, Pallas kernels for 0%

commit v1 on v0

--- a/solution.py
+++ b/solution.py
@@ -7,6 +7,18 @@
 V_DEV = 512
 CH_MB = 8
 NDOC = 8
+
+
+def pass_streams(field_in):
+    return jnp.concatenate(
+        lax.all_to_all(
+            jnp.stack([field_in] * lax.axis_size(("dp", "mp")), 0),
+            axis_name=("dp", "mp"),
+            split_axis=0,
+            concat_axis=0,
+        ),
+        1,
+    )
 
 
 def saturate(logits):
@@ -65,7 +77,7 @@
     token_grad = jnp.dot(table, pooled_grad, precision=lax.Precision.HIGHEST)
     grad_scale = math.sqrt(vocab) * span / math.sqrt(segments * tok_mb)
     logit_grad = (token_grad * slope(block) * grad_scale).astype(jnp.bfloat16)
-    rows = lax.all_gather(normed, ("dp", "mp"), axis=1, tiled=True)[0]
+    rows = pass_streams(normed)[0]
     summed = lax.dot_general(
         rows, logit_grad, (((0,), (0,)), ((), ())), preferred_element_type=jnp.float32
     )

time: 1000 us -> 1060 us (1.060)
  starting transfers between devices: 0.12 us -> 26.8 us
  waiting for transfers between devices: 367 us -> 392 us
  local copies, waits for them, and re-layouts: 0.66 us -> 13.5 us
    all_to_all x0 -> x1, starting transfers between devices: none -> 26.5 us  [pass_streams(): lax.all_to_all(jnp.stack([field_in] * lax.axis_size(('dp', 'mp')), 0), ax...]
    all_gather x1, waiting for transfers between devices: 217 us -> 243 us  [shards(): rows = lax.all_gather(normed, ('dp', 'mp'), axis=1, tiled=True)[0]]
    another operation x0 -> x2, local copies, waits for them, and re-layouts: none -> 13.4 us  [the longest x1 7.21 us: shards(): rows = pass_streams(normed)[0]]
  transfers between devices with their start and end apart: 3 -> 4, of which waited for: 3 -> 3; matrix products, arithmetic and copies ran while one was open for 0% -> 1% of each run, Pallas kernels for 0% -> 0%
where the time goes in v1:
time: 1060 us
  blocking collectives  588 us (55%)
  waiting for transfers between devices  392 us (37%)
  starting transfers between devices  26.8 us (3%)
  matrix products  18.8 us (2%)
  between operations  13.8 us (1%)
  local copies, waits for them, and re-layouts  13.5 us (1%)
    psum x1, blocking collectives, shards(): scores = lax.psum(terms, ('dp', 'mp')) * scale  577 us
    all_gather x1, waiting for transfers between devices, shards(): rows = lax.all_gather(normed, ('dp', 'mp'), axis=1, tiled=True)[0]  243 us
    reduce_scatter x1, waiting for transfers between devices, shards(): lax.psum_scatter(summed.astype(jnp.bfloat16), 'segment', scatter_dimensio...  120 us
    all_gather x1, waiting for transfers between devices, shards(): head_full = lax.all_gather(head, 'segment', axis=0, tiled=True)  27.2 us
    all_to_all x1, starting transfers between devices, pass_streams(): lax.all_to_all(jnp.stack([field_in] * lax.axis_size(('dp', 'mp')), 0), ax...  26.5 us
  transfers between devices with their start and end apart: 4, of which 3 were waited for; matrix products, arithmetic and copies ran while one was open for 1% of the time, Pallas kernels for 0%

profile of v1, /device:TPU:1, one launch (start us, length us, event | category | flops | bytes accessed | tf_op | source)
XLA Modules:
  0.0 1055.4 jit_solution(17185608308409426427)
XLA Ops:
  7.2 0.9 multiply_reduce_fusion
  8.0 0.8 multiply_convert_fusion
  8.9 6.2 stack.2
  15.1 26.5 %all-to-all-start = ((bf16[256,1,2,4096]{3,2,1,0:T(2,128)(2,1)}), bf16[256,1,2,4096]{3,2,1,0:T(2,128)(2,1)}, u32[]{:S(2)}, u32[]{:S(2)}) async-start(bf16[256,1,2,4096]{3,2,1,0:T(2,128)(2,1)} %stack.2), calls=%async_computation | async-start | bytes 8388608 | tf_op jit(solution)/shard_map/all_to_all | solution.py:14
  41.7 0.0 all-gather.5.cloned.1.call-start
  41.8 0.7 all-gather.5.cloned.1.call-update
  42.4 0.0 all-gather.3.cloned.1.call-start
  42.5 0.7 all-gather.3.cloned.1.call-update
  43.2 0.2 reduce-scatter.2.cloned.1.call-start
  43.4 0.2 reduce-window.8
  43.6 0.1 pad_add_fusion
  43.7 27.2 %all-gather.5.cloned.1.call-done = bf16[4096,512]{1,0:T(8,128)(2,1)} async-done(((bf16[2048,512]{1,0:T(8,128)(2,1)}), bf16[4096,512]{1,0:T(8,128)(2,1)}) %all-gather.5.cloned.1.call-update) | async-done | bytes 4194320 | tf_op jit(solution)/shard_map/all_gather | solution.py:53
  70.9 243.1 %all-gather.3.cloned.1.call-done = bf16[1,512,4096]{2,0,1:T(2,128)(2,1)} async-done(((bf16[1,2,4096]{2,0,1:T(2,128)(2,1)}), bf16[1,512,4096]{2,0,1:T(2,128)(2,1)}) %all-gather.3.cloned.1.call-update) | async-done | bytes 4194320 | tf_op jit(solution)/shard_map/all_gather | solution.py:63
  314.0 9.3 fusion
  323.3 1.4 fusion.5
  324.7 11.3 %psum.14 = f32[8,512]{1,0:T(8,128)S(1)} all-reduce(f32[8,512]{1,0:T(8,128)S(1)} %fusion.5), channel_id=1, replica_groups=mesh['dp'=64,'segment'=2,'mp'=4] {'segment'}, use_global_device_ids=true, to_apply=%region_2.3 | all-reduce | flops 4096 | bytes 32768 | tf_op jit(solution)/shard_map/psum | solution.py:68
  335.9 0.1 convolution_bitcast_fusion
  336.1 576.9 %psum.15 = f32[8,8]{0,1:T(8,128)S(1)} all-reduce(f32[8,8]{0,1:T(8,128)S(1)} %convolution_bitcast_fusion), channel_id=1, replica_groups=mesh['dp'=64,'segment'=2,'mp'=4] {'dp','mp'}, use_global_device_ids=true, to_apply=%region_3.4 | all-reduce | flops 64 | bytes 512 | tf_op jit(solution)/shard_map/psum | solution.py:70
  913.0 0.6 subtract_reduce_fusion
  913.6 0.1 convolution_multiply_fusion.1
  913.8 1.4 fusion.4
  915.1 7.2 squeeze_reshape.3
  922.4 6.5 convolution_convert_fusion
  928.9 119.9 %reduce-scatter.2.cloned.1.call-done = bf16[2048,512]{1,0:T(8,128)(2,1)} async-done(((bf16[4096,512]{1,0:T(8,128)(2,1)}), bf16[2048,512]{1,0:T(8,128)(2,1)}) %reduce-scatter.2.cloned.1.call-update) | async-done | bytes 2097168 | tf_op jit(solution)/shard_map/reduce_scatter | solution.py:84
  (15 shorter events, 0.1 us)
Async XLA Ops:
  7.2 328.8 %copy-start = (bf16[8,512]{1,0:T(8,128)(2,1)S(1)}, bf16[8,512]{1,0:T(8,128)(2,1)}, u32[]{:S(2)}) copy-start(bf16[8,512]{1,0:T(8,128)(2,1)} %param.9) | copy-start | bytes 24580
  8.9 6.3 copy-start.1
  15.1 28.3 %copy-start.3 = (s32[8]{0:T(128)S(1)}, s32[8]{0:T(128)}, u32[]{:S(2)}) copy-start(s32[8]{0:T(128)} %param.10) | copy-start | bytes 100
  15.1 900.0 %all-to-all-start = ((bf16[256,1,2,4096]{3,2,1,0:T(2,128)(2,1)}), bf16[256,1,2,4096]{3,2,1,0:T(2,128)(2,1)}, u32[]{:S(2)}, u32[]{:S(2)}) async-start(bf16[256,1,2,4096]{3,2,1,0:T(2,128)(2,1)} %stack.2), calls=%async_computation | async-start | bytes 8388608 | tf_op jit(solution)/shard_map/all_to_all | solution.py:14
  41.7 29.2 %all-gather.5.cloned.1.call-start = ((), (), s32[]{:S(2)}) async-start(), calls=%async_computation.3 | async-start | bytes 6291456 | tf_op jit(solution)/shard_map/all_gather | solution.py:53
  42.4 271.6 %all-gather.3.cloned.1.call-start = ((), (), s32[]{:S(2)}) async-start(), calls=%async_computation.2 | async-start | bytes 8421376 | tf_op jit(solution)/shard_map/all_gather | solution.py:63
  43.2 1005.7 %reduce-scatter.2.cloned.1.call-start = ((), (), s32[]{:S(2)}) async-start(), calls=%async_computation.4 | async-start | bytes 6291456 | tf_op jit(solution)/shard_map/reduce_scatter | solution.py:84
  43.7 869.3 %copy-start.2 = (s32[8]{0:T(128)S(1)}, s32[8]{0:T(128)}, u32[]{:S(2)}) copy-start(s32[8]{0:T(128)} %param.11) | copy-start | bytes 100
Sparse Core Ops, SparseCore 0:
  44.6 26.2 all-gather.4
  76.1 237.9 all-gather.2
  929.1 119.7 reduce-scatter.1
